TPU v7x, 32 devices: a whole 2x2x4 slice. The times are simulated.
32 devices in a mesh: pitch: 4 (over y, core), span: 8 (over z, x).
Axes of the slice: x: 2, y: 2, z: 4, core: 2. Of those that a mesh axis runs over, the one named last changes fastest.
Arguments:
- flow_state: float32 [4, 128, 512, 256], P(None, 'pitch', 'span'), may hold values from -6 to 6
- wall_inverse: float32 [64, 64], replicated, as said below
- metal_inverse: float32 [16, 16], replicated, as said below
- metal_state: float32 [16, 65536], P(None, ('pitch', 'span')), may hold values from -6 to 6
- metal_conduct: float32 [65536], P(('pitch', 'span')), may hold values from 0.3 to 3
- face_coef: float32 [2, 32768], P(None, ('pitch', 'span')), may hold values from 0.3 to 3
- owner_map: int32 [32768, 1], P(('pitch', 'span')), may hold values from 0 to 31; in each aligned block of 1024 rows (0 to 1023, 1024 to 2047, ...) at most 64 rows name the same one
- face_cell: int32 [32768], P(('pitch', 'span')), may hold values from 0 to 2047
- sample_col: int32 [32768], P(('pitch', 'span')), may hold values from 0 to 2047
- sample_low: int32 [32768], P(('pitch', 'span')), may hold values from 0 to 192
Outputs:
- new_state: float32 [4, 128, 512, 256], P(None, 'pitch', 'span')
- metal_out: float32 [16, 65536], P(None, ('pitch', 'span'))
Inputs may be any that keep to these rules, and one draw needn't show every extreme that they name: `owner_map`: at most 64 faces of one device have the same owner; in every draw some device sends exactly 64 faces to one owner. `face_cell`: columns are numbered pitch cell times 64 plus span cell. `sample_col`: numbered as face_cell. `wall_inverse`: diagonal entries are the largest of their rows, within 0.5 to 1. `metal_inverse`: diagonal entries are the largest of their rows, within 0.5 to 1.
All inputs are finite; a program needn't handle non-finite values.
Results may differ from a plain program's by a relative error of at most 0.0001.
Values sent between devices are 32-bit elements; how exact they have to be, the bound alone decides.
A program may use at most 128 MiB of HBM per device.

v0:
```python
import functools
import jax
import jax.numpy as jnp
from jax import lax
from jax.experimental import pallas as pl
from jax.experimental.pallas import tpu as pltpu
from jax.sharding import PartitionSpec as P

PICARD = 3
ALPHA_FLUID = 0.5
BETA_METAL = 0.5
DRAG_COEF = 0.5
TIME_STEP = 0.5
DIFFUSION = 0.2
ADVECTION = 0.6
HALF = 64
LANES = 128
F32 = jnp.float32
BF16 = jnp.bfloat16
VMEM_LIMIT = 56 * 1024 * 1024
MESH = pl.DeviceIdType.MESH

NN = (((1,), (0,)), ((), ()))
NT = (((1,), (1,)), ((), ()))
TN = (((0,), (0,)), ((), ()))


def pieces(value, count):
    out = []
    for _ in range(count):
        part = value.astype(BF16)
        out.append(part)
        value = value - part.astype(F32)
    return out


def dot(a, b, dims):
    return lax.dot_general(a, b, dims, preferred_element_type=F32)


def dot3(a, b, dims):
    (a1, a2), (b1, b2) = (a, b)
    return dot(a1, b1, dims) + (dot(a1, b2, dims) + dot(a2, b1, dims))


def onehot(row, count, mask=None):
    index = lax.broadcasted_iota(jnp.int32, (count, row.shape[1]), 0)
    if mask is not None:
        index = index & mask
    return jnp.where(index == row, 1.0, 0.0).astype(F32)


def sample_kernel(
    devices,
    per_peer,
    span_cells,
    col_ref,
    metal_inv_ref,
    x_ref,
    low_ref,
    owner_ref,
    coef_ref,
    g_ref,
    metal_ref,
    conduct_ref,
    send_ref,
    faces_ref,
    edge_ref,
    xv,
    rows,
    gg,
    sem,
):
    comps = x_ref.shape[0]
    columns = x_ref.shape[1]
    pitch_cells = columns // span_cells
    faces = rows.shape[1]
    loads = [pltpu.make_async_copy(x_ref.at[c], xv.at[c], sem.at[c]) for c in range(comps)]
    for load in loads:
        load.start()
    gg[...] = jnp.zeros_like(gg)
    gg[0:HALF, 0:HALF] = g_ref[...]
    gg[HALF:LANES, HALF:LANES] = g_ref[...]
    table = pieces(gg[...], 2)
    row_pick = lax.broadcasted_iota(jnp.int32, (8, LANES), 0)
    lane_pick = lax.broadcasted_iota(jnp.int32, (8, LANES), 1)
    top_u = jnp.broadcast_to(gg[0:1, :], (8, LANES))
    top_w = jnp.broadcast_to(gg[HALF : HALF + 1, :], (8, LANES))
    top = pieces(jnp.where(row_pick == 0, top_u, jnp.where(row_pick == 1, top_w, 0.0)), 2)

    owner = owner_ref[...]
    choose = onehot(owner, devices)
    choose_b = choose.astype(BF16)
    up_row = lax.broadcasted_iota(jnp.int32, (LANES, LANES), 0)
    up_col = lax.broadcasted_iota(jnp.int32, (LANES, LANES), 1)
    upper = jnp.where(up_row < up_col, 1.0, 0.0).astype(BF16)
    running = jnp.zeros((devices, 1), F32)
    ranks = []
    for start in range(0, faces, LANES):
        block = choose[:, start : start + LANES]
        prior = dot(choose_b[:, start : start + LANES], upper, NN) + running
        ranks.append(jnp.sum(prior * block, axis=0, keepdims=True))
        running = running + jnp.sum(block, axis=1, keepdims=True)
    rank = jnp.concatenate(ranks, axis=1)

    free_top = jnp.zeros(metal_ref.shape[1:], F32)
    for i in range(metal_ref.shape[0]):
        free_top = free_top + metal_inv_ref[0, i] * metal_ref[i]

    for load in loads:
        load.wait()

    def gather(group, carry):
        base = pl.multiple_of(group * 8, 8)
        for k in range(8):
            col = col_ref[base + k]
            for c in range(3):
                rows[c, pl.ds(base + k, 1), :] = xv[c, pl.ds(col, 1), :]
        return carry

    lax.fori_loop(0, faces // 8, gather, 0)
    for side in range(2):
        for c in range(comps):
            for p in range(pitch_cells):
                at = p * span_cells + side * (span_cells - 1)
                edge_ref[side, c, p : p + 1, :] = xv[c, at : at + 1, :]

    lane = lax.broadcasted_iota(jnp.int32, (LANES, LANES), 1)
    for part in range(faces // LANES):
        at = slice(part * LANES, (part + 1) * LANES)
        low = jnp.broadcast_to(low_ref[part : part + 1, :], (LANES, LANES)).T
        index = low + (lane & (HALF - 1))
        far = index >= LANES
        index = index & (LANES - 1)

        def window(c):
            near = jnp.take_along_axis(rows[c, at, 0:LANES], index, axis=1)
            return jnp.where(
                far, jnp.take_along_axis(rows[c, at, LANES : 2 * LANES], index, axis=1), near
            )

        force = jnp.where(lane < HALF, window(0), window(1))
        speed = dot3(pieces(force, 2), table, NT)
        for step in range(PICARD):
            square = speed * speed
            damping = DRAG_COEF * lax.rsqrt(1.0 + square + pltpu.roll(square, HALF, 1))
            rest = pieces(force - damping * speed, 2)
            if step < PICARD - 1:
                speed = dot3(rest, table, NT)
        top_speed = dot3(top, rest, NT)
        fluid_top = dot3(top, pieces(window(2), 2), NT)
        conduct = coef_ref[0:1, at]
        viscosity = coef_ref[1:2, at]
        faces_ref[0:1, at] = viscosity * top_speed[0:1]
        faces_ref[1:2, at] = viscosity * top_speed[1:2]
        faces_ref[2:3, at] = fluid_top[0:1]
        faces_ref[3:4, at] = conduct
    faces_ref[4:5, :] = owner.astype(F32)
    faces_ref[5:6, :] = rank
    faces_ref[6:8, :] = jnp.zeros((2, faces), F32)

    conduct = faces_ref[3:4, :]
    heat = conduct * faces_ref[2:3, :]
    place = onehot(rank.astype(jnp.int32), HALF).astype(BF16)

    def slots(value, count):
        total = jnp.zeros((devices, HALF), F32)
        for part in pieces(value, count):
            total = total + dot((choose * part.astype(F32)).astype(BF16), place, NT)
        return total

    used = slots(jnp.ones_like(rank), 1)
    blank = jnp.zeros((devices, HALF), F32)

    def widen(value):
        if per_peer == HALF:
            return value
        return jnp.concatenate([value, jnp.zeros((devices, HALF - per_peer), F32)], axis=1)

    send_ref[pl.ds(0, devices, stride=8), :] = jnp.concatenate(
        [slots(heat, 3), slots(conduct, 3)], axis=1
    )
    send_ref[pl.ds(1, devices, stride=8), :] = jnp.concatenate([used, blank], axis=1)
    send_ref[pl.ds(2, devices, stride=8), :] = jnp.concatenate(
        [widen(free_top), widen(conduct_ref[...])], axis=1
    )
    empty = jnp.concatenate([blank, blank], axis=1)
    for j in range(3, 8):
        send_ref[pl.ds(j, devices, stride=8), :] = empty


def exchange_kernel(
    n_pitch,
    n_span,
    x_ref,
    edge_ref,
    tile_ref,
    got_ref,
    pitch_ref,
    span_ref,
    own_sem,
    tile_send,
    tile_recv,
    halo_send,
    halo_recv,
):
    devices = n_pitch * n_span
    pitch = lax.axis_index("pitch")
    span = lax.axis_index("span")
    me = pitch * n_span + span
    rows = x_ref.shape[1]
    barrier = pltpu.get_barrier_semaphore()

    def greet(k, carry):
        peer = lax.rem(me + k, devices)
        pl.semaphore_signal(
            barrier, inc=1, device_id=(peer // n_span, lax.rem(peer, n_span)), device_id_type=MESH
        )
        return carry

    lax.fori_loop(1, devices, greet, 0)
    pl.semaphore_wait(barrier, devices - 1)

    after = (lax.rem(pitch + 1, n_pitch), span)
    before = (lax.rem(pitch + n_pitch - 1, n_pitch), span)
    up = pltpu.make_async_remote_copy(
        src_ref=x_ref.at[:, rows - 1], dst_ref=pitch_ref.at[0], send_sem=halo_send.at[0],
        recv_sem=halo_recv.at[0], device_id=after, device_id_type=MESH,
    )
    down = pltpu.make_async_remote_copy(
        src_ref=x_ref.at[:, 0], dst_ref=pitch_ref.at[1], send_sem=halo_send.at[1],
        recv_sem=halo_recv.at[1], device_id=before, device_id_type=MESH,
    )
    right = pltpu.make_async_remote_copy(
        src_ref=edge_ref.at[1], dst_ref=span_ref.at[0], send_sem=halo_send.at[2],
        recv_sem=halo_recv.at[2], device_id=(pitch, lax.rem(span + 1, n_span)),
        device_id_type=MESH,
    )
    left = pltpu.make_async_remote_copy(
        src_ref=edge_ref.at[0], dst_ref=span_ref.at[1], send_sem=halo_send.at[3],
        recv_sem=halo_recv.at[3], device_id=(pitch, lax.rem(span + n_span - 1, n_span)),
        device_id_type=MESH,
    )
    up.start()
    down.start()

    @pl.when(span < n_span - 1)
    def _():
        right.start()

    @pl.when(span > 0)
    def _():
        left.start()

    def tile_copy(k):
        peer = lax.rem(me + k, devices)
        return pltpu.make_async_remote_copy(
            src_ref=tile_ref.at[pl.ds(pl.multiple_of(peer * 8, 8), 8), :],
            dst_ref=got_ref.at[pl.ds(pl.multiple_of(me * 8, 8), 8), :],
            send_sem=tile_send.at[k],
            recv_sem=tile_recv.at[k],
            device_id=(peer // n_span, lax.rem(peer, n_span)),
            device_id_type=MESH,
        )

    def tile_start(k, carry):
        tile_copy(k).start()
        return carry

    lax.fori_loop(1, devices, tile_start, 0)
    mine = pl.ds(pl.multiple_of(me * 8, 8), 8)
    own = pltpu.make_async_copy(tile_ref.at[mine, :], got_ref.at[mine, :], own_sem)
    own.start()

    @pl.when(span == 0)
    def _():
        span_ref[0] = jnp.zeros(span_ref.shape[1:], F32)

    @pl.when(span == n_span - 1)
    def _():
        span_ref[1] = jnp.zeros(span_ref.shape[1:], F32)

    own.wait()

    def tile_wait(k, carry):
        tile_copy(k).wait()
        return carry

    lax.fori_loop(1, devices, tile_wait, 0)
    up.wait()
    down.wait()

    @pl.when(span < n_span - 1)
    def _():
        right.wait_send()

    @pl.when(span > 0)
    def _():
        left.wait_send()

    @pl.when(span > 0)
    def _():
        right.wait_recv()

    @pl.when(span < n_span - 1)
    def _():
        left.wait_recv()


def advance_kernel(
    devices,
    per_peer,
    g_ref,
    metal_inv_ref,
    x_ref,
    prev_ref,
    next_ref,
    pitch_ref,
    span_ref,
    faces_ref,
    cell_ref,
    got_ref,
    metal_ref,
    conduct_ref,
    out_ref,
    metal_out_ref,
    wall,
):
    comp = pl.program_id(0)
    part = pl.program_id(1)
    parts = pl.num_programs(1)
    chunk, span_cells, normal = x_ref.shape[1:]
    pitch_cells = wall.shape[1] // 4
    fluid_factor = 1.0 - ALPHA_FLUID * g_ref[0, 0]
    metal_factor = 1.0 - BETA_METAL * metal_inv_ref[0, 0]

    @pl.when((comp == 0) & (part == 0))
    def _():
        rank = faces_ref[5:6, :].astype(jnp.int32)
        choose = onehot(faces_ref[4:5, :].astype(jnp.int32), devices).astype(BF16)
        picked = jnp.zeros((LANES, rank.shape[1]), F32)
        for piece in pieces(got_ref[pl.ds(2, devices, stride=8), :], 3):
            picked = picked + dot(piece, choose, TN)
        picked = picked * onehot(rank, LANES, HALF - 1)
        metal_top = jnp.sum(picked[0:HALF], axis=0, keepdims=True)
        conduct_metal = jnp.sum(picked[HALF:LANES], axis=0, keepdims=True)
        fluid_top = faces_ref[2:3, :]
        conduct = faces_ref[3:4, :]
        wall_temp = (conduct * fluid_top + conduct_metal * metal_top) / (
            conduct * fluid_factor + conduct_metal * metal_factor
        )
        heat = conduct * (fluid_top - fluid_factor * wall_temp)
        cell = cell_ref[...]
        at_pitch = onehot(cell // span_cells, pitch_cells)
        at_span = onehot(lax.rem(cell, span_cells), span_cells).astype(BF16)
        split = [pieces(v, 3) for v in (faces_ref[0:1, :], faces_ref[1:2, :], heat)]
        total = jnp.zeros(wall.shape, F32)
        for k in range(3):
            spread = [(at_pitch * s[k].astype(F32)).astype(BF16) for s in split]
            spread.append(jnp.zeros(at_pitch.shape, BF16))
            total = total + dot(at_span, jnp.concatenate(spread, axis=0), NT)
        wall[...] = -TIME_STEP * total

        first = got_ref[pl.ds(0, devices, stride=8), :]
        used = got_ref[pl.ds(1, devices, stride=8), :][:, 0:per_peer]
        flux = first[:, 0:per_peer]
        fluid = first[:, HALF : HALF + per_peer]
        metal_k = conduct_ref[...]
        order = metal_ref.shape[0]
        old = [metal_ref[i] for i in range(order)]

        def free(k):
            value = metal_inv_ref[k, 0] * old[0]
            for i in range(1, order):
                value = value + metal_inv_ref[k, i] * old[i]
            return value

        top = free(0)
        temp = (flux + metal_k * top) / (
            fluid * fluid_factor + metal_k * metal_factor + (1.0 - used)
        )
        for k in range(order):
            value = top if k == 0 else free(k)
            metal_out_ref[k] = jnp.where(
                used > 0.5, value + BETA_METAL * temp * metal_inv_ref[k, 0], old[k]
            )

    weight = TIME_STEP * DIFFUSION
    drift = TIME_STEP * ADVECTION * 0.5
    row = lax.broadcasted_iota(jnp.int32, (span_cells, normal), 0)
    lane = lax.broadcasted_iota(jnp.int32, (span_cells, normal), 1)
    lane_one = lax.broadcasted_iota(jnp.int32, (span_cells, LANES), 1)
    before = jnp.where(part == 0, pitch_ref[0, 0], prev_ref[0, 0])
    after = jnp.where(part == parts - 1, pitch_ref[1, 0], next_ref[0, 0])
    for p in range(chunk):
        here = x_ref[0, p]
        prev = before if p == 0 else x_ref[0, p - 1]
        post = after if p == chunk - 1 else x_ref[0, p + 1]
        span_prev = jnp.where(row == 0, span_ref[0, 0, p : p + 1, :], pltpu.roll(here, 1, 0))
        span_next = jnp.where(
            row == span_cells - 1, span_ref[1, 0, p : p + 1, :], pltpu.roll(here, span_cells - 1, 0)
        )
        down = jnp.where(lane == 0, here, pltpu.roll(here, 1, 1))
        up = jnp.where(lane == normal - 1, here, pltpu.roll(here, normal - 1, 1))
        value = (
            (1.0 - 6.0 * weight) * here
            + (weight - drift) * post
            + (weight + drift) * prev
            + weight * ((span_prev + span_next) + (down + up))
        )
        out_ref[0, p] = value
        column = comp * pitch_cells + part * chunk + p
        source = pltpu.roll(wall[...], lax.rem(LANES - column, LANES), 1)
        out_ref[0, p, :, 0:LANES] += jnp.where(lane_one == 0, source, 0.0)


def vmem():
    return pl.BlockSpec(memory_space=pltpu.VMEM)


def smem():
    return pl.BlockSpec(memory_space=pltpu.SMEM)


def local(
    n_pitch,
    n_span,
    flow_state,
    wall_inverse,
    metal_inverse,
    metal_state,
    metal_conduct,
    face_coef,
    owner_map,
    face_cell,
    sample_col,
    sample_low,
):
    devices = n_pitch * n_span
    comps, pitch_cells, span_cells, normal = flow_state.shape
    order, slot_dev = metal_state.shape
    per_peer = slot_dev // devices
    faces = owner_map.shape[0]
    metal = metal_state.reshape(order, devices, per_peer)
    conduct = metal_conduct.reshape(devices, per_peer)
    any_space = pl.BlockSpec(memory_space=pl.ANY)

    tiles, face_rows, edges = pl.pallas_call(
        functools.partial(sample_kernel, devices, per_peer, span_cells),
        out_shape=(
            jax.ShapeDtypeStruct((devices * 8, LANES), F32),
            jax.ShapeDtypeStruct((8, faces), F32),
            jax.ShapeDtypeStruct((2, comps, pitch_cells, normal), F32),
        ),
        in_specs=[smem(), smem(), any_space] + [vmem()] * 6,
        out_specs=[vmem()] * 3,
        scratch_shapes=[
            pltpu.VMEM((comps, pitch_cells * span_cells, normal), F32),
            pltpu.VMEM((3, faces, normal), F32),
            pltpu.VMEM((LANES, LANES), F32),
            pltpu.SemaphoreType.DMA((comps,)),
        ],
        compiler_params=pltpu.CompilerParams(vmem_limit_bytes=VMEM_LIMIT),
        name="sample_faces",
    )(
        sample_col,
        metal_inverse,
        flow_state.reshape(comps, pitch_cells * span_cells, normal),
        sample_low.reshape(faces // LANES, LANES),
        owner_map.reshape(1, faces),
        face_coef,
        wall_inverse,
        metal,
        conduct,
    )

    got, pitch_halo, span_halo = pl.pallas_call(
        functools.partial(exchange_kernel, n_pitch, n_span),
        out_shape=(
            jax.ShapeDtypeStruct((devices * 8, LANES), F32),
            jax.ShapeDtypeStruct((2, comps, span_cells, normal), F32),
            jax.ShapeDtypeStruct((2, comps, pitch_cells, normal), F32),
        ),
        in_specs=[any_space, vmem(), vmem()],
        out_specs=[vmem()] * 3,
        scratch_shapes=[
            pltpu.SemaphoreType.DMA,
            pltpu.SemaphoreType.DMA((devices,)),
            pltpu.SemaphoreType.DMA((devices,)),
            pltpu.SemaphoreType.DMA((4,)),
            pltpu.SemaphoreType.DMA((4,)),
        ],
        compiler_params=pltpu.CompilerParams(
            collective_id=0, has_side_effects=True, vmem_limit_bytes=VMEM_LIMIT
        ),
        name="exchange",
    )(flow_state, edges, tiles)

    chunk = pitch_cells // 2
    new_state, metal_out = pl.pallas_call(
        functools.partial(advance_kernel, devices, per_peer),
        grid=(comps, 2),
        out_shape=(
            jax.ShapeDtypeStruct(flow_state.shape, F32),
            jax.ShapeDtypeStruct(metal.shape, F32),
        ),
        in_specs=[
            smem(),
            smem(),
            pl.BlockSpec((1, chunk, span_cells, normal), lambda c, i: (c, i, 0, 0)),
            pl.BlockSpec(
                (1, 1, span_cells, normal),
                lambda c, i: (c, lax.rem(i * chunk + pitch_cells - 1, pitch_cells), 0, 0),
            ),
            pl.BlockSpec(
                (1, 1, span_cells, normal),
                lambda c, i: (c, lax.rem((i + 1) * chunk, pitch_cells), 0, 0),
            ),
            pl.BlockSpec((2, 1, span_cells, normal), lambda c, i: (0, c, 0, 0)),
            pl.BlockSpec((2, 1, chunk, normal), lambda c, i: (0, c, i, 0)),
            vmem(),
            vmem(),
            vmem(),
            vmem(),
            vmem(),
        ],
        out_specs=[
            pl.BlockSpec((1, chunk, span_cells, normal), lambda c, i: (c, i, 0, 0)),
            pl.BlockSpec(metal.shape, lambda c, i: (0, 0, 0)),
        ],
        scratch_shapes=[pltpu.VMEM((span_cells, 4 * pitch_cells), F32)],
        compiler_params=pltpu.CompilerParams(vmem_limit_bytes=VMEM_LIMIT),
        name="advance",
    )(
        wall_inverse,
        metal_inverse,
        flow_state,
        flow_state,
        flow_state,
        pitch_halo,
        span_halo,
        face_rows,
        face_cell.reshape(1, faces),
        got,
        metal,
        conduct,
    )
    return (new_state, metal_out.reshape(order, slot_dev))


def solution(mesh):
    return jax.shard_map(
        functools.partial(local, mesh.shape["pitch"], mesh.shape["span"]),
        mesh=mesh,
        in_specs=(
            P(None, "pitch", "span", None),
            P(),
            P(),
            P(None, ("pitch", "span")),
            P(("pitch", "span")),
            P(None, ("pitch", "span")),
            P(("pitch", "span"), None),
            P(("pitch", "span")),
            P(("pitch", "span")),
            P(("pitch", "span")),
        ),
        out_specs=(P(None, "pitch", "span", None), P(None, ("pitch", "span"))),
        check_vma=False,
    )
```

profile of v0, /device:TPU:0, one launch (start us, length us, event | category | flops | bytes accessed | tf_op | source)
XLA Modules:
  0.0 56.0 jit_solution(6477660359476179928)
XLA Ops:
  0.6 1.4 %reshape.29.conduct_ref = f32[32,64]{1,0:T(8,128)} reshape(f32[2048]{0:T(1024)} %param.14) | data formatting | bytes 16384 | tf_op jit(solution)/shard_map/reshape | solution.py:445
  2.0 1.7 %reshape.28.metal_ref = f32[16,32,64]{2,1,0:T(8,128)} reshape(f32[16,2048]{1,0:T(8,128)} %param.13) | data formatting | bytes 262144 | tf_op jit(solution)/shard_map/reshape | solution.py:444
  3.7 19.3 %sample_faces.1 = (f32[256,128]{1,0:T(8,128)}, f32[8,1024]{1,0:T(8,128)}, f32[2,4,32,256]{3,2,1,0:T(8,128)}) custom-call(s32[1024]{0:T(1024)} %col_ref.1, f32[16,16]{1,0:T(8,128)} %metal_inv_ref.3, f32[4,2048,256]{2,1,0:T(8,128)} %bitcast.4, s32[8,128]{1,0:T(8,128)} %bitcast.5, s32[1,1024]{1,0:T(1,128)} %bitcast.6, f32[2,1024]{1,0:T(2,128)} %coef_ref.1, ...), custom_call_target="tpu_custom_call" | custom-call | tf_op jit(solution)/shard_map/sample_faces/pallas_call | solution.py:448
  23.0 18.3 %exchange.1 = (f32[256,128]{1,0:T(8,128)}, f32[2,4,64,256]{3,2,1,0:T(8,128)}, f32[2,4,32,256]{3,2,1,0:T(8,128)}) custom-call(f32[4,32,64,256]{3,2,1,0:T(8,128)} %next_ref.1, f32[2,4,32,256]{3,2,1,0:T(8,128)} %get-tuple-element.10.edge_ref, f32[256,128]{1,0:T(8,128)} %get-tuple-element.11.tile_ref), custom_call_target="tpu_custom_call" | custom-call | tf_op jit(solution)/shard_map/exchange/pallas_call | solution.py:477
  41.3 13.0 %advance.1 = (f32[4,32,64,256]{3,2,1,0:T(8,128)}, f32[16,32,64]{2,1,0:T(8,128)}) custom-call(f32[64,64]{1,0:T(8,128)} %g_ref.3, f32[16,16]{1,0:T(8,128)} %metal_inv_ref.3, f32[4,32,64,256]{3,2,1,0:T(8,128)} %next_ref.1, f32[4,32,64,256]{3,2,1,0:T(8,128)} %next_ref.1, f32[4,32,64,256]{3,2,1,0:T(8,128)} %next_ref.1, ...), custom_call_target="tpu_custom_call" | custom-call | tf_op jit(solution)/shard_map/advance/pallas_call | solution.py:500
  54.3 1.7 %reshape.31 = f32[16,2048]{1,0:T(8,128)} reshape(f32[16,32,64]{2,1,0:T(8,128)} %get-tuple-element.17) | data formatting | bytes 262144 | tf_op jit(solution)/shard_map/reshape | solution.py:548
where the time goes:
time: 56.5 us; the launch traced here: 56 us
  Pallas kernels  50.6 us (90%)
  local copies, waits for them, and re-layouts  4.78 us (8%)
  between operations  0.65 us (1%)
    pallas_call x1, Pallas kernels, local(): pl.pallas_call(functools.partial(sample_kernel, devices, per_peer, span_c...  19.3 us
    pallas_call x1, Pallas kernels, local(): pl.pallas_call(functools.partial(exchange_kernel, n_pitch, n_span), out_s...  18.3 us
    pallas_call x1, Pallas kernels, local(): pl.pallas_call(functools.partial(advance_kernel, devices, per_peer), grid...  13 us
    reshape x1, local copies, waits for them, and re-layouts, local(): return (new_state, metal_out.reshape(order, slot_dev))  1.72 us
    reshape x1, local copies, waits for them, and re-layouts, local(): metal = metal_state.reshape(order, devices, per_peer)  1.7 us
    reshape x1, local copies, waits for them, and re-layouts, local(): conduct = metal_conduct.reshape(devices, per_peer)  1.37 us

commit v1 on v0

v1 whole, which is shorter than its diff:
```python
import functools
import jax
import jax.numpy as jnp
from jax import lax
from jax.experimental import pallas as pl
from jax.experimental.pallas import tpu as pltpu
from jax.sharding import PartitionSpec as P

PICARD = 3
ALPHA_FLUID = 0.5
BETA_METAL = 0.5
DRAG_COEF = 0.5
TIME_STEP = 0.5
DIFFUSION = 0.2
ADVECTION = 0.6
HALF = 64
LANES = 128
F32 = jnp.float32
BF16 = jnp.bfloat16
VMEM_LIMIT = 56 * 1024 * 1024
MESH = pl.DeviceIdType.MESH

NN = (((1,), (0,)), ((), ()))
NT = (((1,), (1,)), ((), ()))
TN = (((0,), (0,)), ((), ()))


def pieces(value, count):
    out = []
    for _ in range(count):
        part = value.astype(BF16)
        out.append(part)
        value = value - part.astype(F32)
    return out


def dot(a, b, dims):
    return lax.dot_general(a, b, dims, preferred_element_type=F32)


def dot3(a, b, dims):
    (a1, a2), (b1, b2) = (a, b)
    return dot(a1, b1, dims) + (dot(a1, b2, dims) + dot(a2, b1, dims))


def onehot(row, count, mask=None):
    index = lax.broadcasted_iota(jnp.int32, (count, row.shape[1]), 0)
    if mask is not None:
        index = index & mask
    return jnp.where(index == row, 1.0, 0.0).astype(F32)


def sample_kernel(
    n_pitch,
    n_span,
    per_peer,
    span_cells,
    col_ref,
    low_smem,
    g_smem,
    metal_smem,
    x_ref,
    low_ref,
    owner_ref,
    cell_ref,
    coef_ref,
    g_ref,
    metal_inv_ref,
    metal_ref,
    conduct_ref,
    wall_ref,
    metal_out_ref,
    pitch_ref,
    span_ref,
    xv,
    rows,
    gg,
    speed_rows,
    edges,
    offer,
    offer_got,
    reply,
    reply_got,
    slot_rows,
    load_sem,
    tile_send,
    tile_recv,
    halo_send,
    halo_recv,
):
    devices = n_pitch * n_span
    pitch = lax.axis_index("pitch")
    span = lax.axis_index("span")
    me = pitch * n_span + span
    comps = x_ref.shape[0]
    columns = x_ref.shape[1]
    pitch_cells = columns // span_cells
    faces = rows.shape[1]
    slot_dev = metal_ref.shape[1]
    per_tile = LANES // per_peer
    barrier = pltpu.get_barrier_semaphore()

    def wrap(value, size):
        return jnp.where(value >= size, value - size, value)

    def each_peer(visit):
        for d in range(1, n_span):
            visit(pitch, wrap(span + d, n_span))

        def ring(step, carry):
            other = wrap(pitch + step, n_pitch)
            for d in range(n_span):
                visit(other, wrap(span + d, n_span))
            return carry

        lax.fori_loop(1, n_pitch, ring, 0)

    each_peer(
        lambda p, s: pl.semaphore_signal(barrier, inc=1, device_id=(p, s), device_id_type=MESH)
    )
    loads = [
        pltpu.make_async_copy(
            x_ref.at[c, :, pl.ds(t * LANES, LANES)], xv.at[c, t], load_sem.at[c, t]
        )
        for c in range(comps)
        for t in range(2)
    ]
    for load in loads:
        load.start()

    old = metal_ref[...]
    free = dot3(pieces(metal_inv_ref[...], 2), pieces(old, 2), NN)
    offer[0:1, :] = free[0:1]
    offer[1:2, :] = conduct_ref[...]
    offer[2:8, :] = jnp.zeros((6, slot_dev), F32)

    pl.semaphore_wait(barrier, devices - 1)
    up = pltpu.make_async_remote_copy(
        src_ref=x_ref.at[:, pl.ds(columns - span_cells, span_cells)], dst_ref=pitch_ref.at[0],
        send_sem=halo_send.at[0], recv_sem=halo_recv.at[0],
        device_id=(wrap(pitch + 1, n_pitch), span), device_id_type=MESH,
    )
    down = pltpu.make_async_remote_copy(
        src_ref=x_ref.at[:, pl.ds(0, span_cells)], dst_ref=pitch_ref.at[1],
        send_sem=halo_send.at[1], recv_sem=halo_recv.at[1],
        device_id=(wrap(pitch + n_pitch - 1, n_pitch), span), device_id_type=MESH,
    )
    right = pltpu.make_async_remote_copy(
        src_ref=edges.at[1], dst_ref=span_ref.at[0],
        send_sem=halo_send.at[2], recv_sem=halo_recv.at[2],
        device_id=(pitch, wrap(span + 1, n_span)), device_id_type=MESH,
    )
    left = pltpu.make_async_remote_copy(
        src_ref=edges.at[0], dst_ref=span_ref.at[1],
        send_sem=halo_send.at[3], recv_sem=halo_recv.at[3],
        device_id=(pitch, wrap(span + n_span - 1, n_span)), device_id_type=MESH,
    )
    up.start()
    down.start()
    mine = pl.ds(pl.multiple_of(me * 8, 8), 8)

    def offer_of(index):
        return offer.at[:, pl.ds(pl.multiple_of(index // per_tile * LANES, LANES), LANES)]

    def offer_start(p, s):
        pltpu.make_async_remote_copy(
            src_ref=offer_of(p * n_span + s), dst_ref=offer_got.at[mine, :],
            send_sem=tile_send.at[0], recv_sem=tile_recv.at[0],
            device_id=(p, s), device_id_type=MESH,
        ).start()

    each_peer(offer_start)
    offer_got[mine, :] = offer[
        :, pl.ds(pl.multiple_of(me // per_tile * LANES, LANES), LANES)
    ]

    gg[...] = jnp.zeros_like(gg)
    gg[0:HALF, 0:HALF] = g_ref[...]
    gg[HALF:LANES, HALF:LANES] = g_ref[...]
    table_hi, table_lo = pieces(gg[...], 2)
    both = jnp.concatenate([table_hi, table_hi], axis=1)
    single = jnp.concatenate([table_lo, jnp.zeros_like(table_lo)], axis=1)
    table = jnp.concatenate([both, single], axis=0)
    row_pick = lax.broadcasted_iota(jnp.int32, (8, LANES), 0)
    top_u = jnp.broadcast_to(gg[0:1, :], (8, LANES))
    top_w = jnp.broadcast_to(gg[HALF : HALF + 1, :], (8, LANES))
    top = pieces(jnp.where(row_pick == 0, top_u, jnp.where(row_pick == 1, top_w, 0.0)), 2)

    choose = onehot(owner_ref[...], devices)
    choose_b = choose.astype(BF16)
    up_row = lax.broadcasted_iota(jnp.int32, (LANES, LANES), 0)
    up_col = lax.broadcasted_iota(jnp.int32, (LANES, LANES), 1)
    upper = jnp.where(up_row < up_col, 1.0, 0.0).astype(BF16)
    running = jnp.zeros((devices, 1), F32)
    ranks = []
    for start in range(0, faces, LANES):
        block = choose[:, start : start + LANES]
        prior = dot(choose_b[:, start : start + LANES], upper, NN) + running
        ranks.append(jnp.sum(prior * block, axis=0, keepdims=True))
        running = running + jnp.sum(block, axis=1, keepdims=True)
    lane_at = (me & (per_tile - 1)) * per_peer
    rank = jnp.concatenate(ranks, axis=1).astype(jnp.int32) + lane_at
    place = onehot(rank, LANES)
    place_b = place.astype(BF16)

    for load in loads:
        load.wait()

    for side in range(2):
        for c in range(comps):
            for p in range(pitch_cells):
                at = p * span_cells + side * (span_cells - 1)
                for t in range(2):
                    edges[side, c, p : p + 1, t * LANES : (t + 1) * LANES] = xv[c, t, at : at + 1, :]

    @pl.when(span < n_span - 1)
    def _():
        right.start()

    @pl.when(span > 0)
    def _():
        left.start()

    @pl.when(span == 0)
    def _():
        span_ref[0] = jnp.zeros(span_ref.shape[1:], F32)

    @pl.when(span == n_span - 1)
    def _():
        span_ref[1] = jnp.zeros(span_ref.shape[1:], F32)

    lane_row = lax.broadcasted_iota(jnp.int32, (1, LANES), 1)

    def gather(group, carry):
        base = pl.multiple_of(group * 8, 8)
        for k in range(8):
            col = col_ref[base + k]
            low = low_smem[base + k]
            near = low >> 7
            far = (low + HALF - 1) >> 7
            keep = lane_row >= (low & (LANES - 1))
            for c in range(3):
                rows[c, pl.ds(base + k, 1), :] = jnp.where(
                    keep, xv[c, near, pl.ds(col, 1), :], xv[c, far, pl.ds(col, 1), :]
                )
        return carry

    lax.fori_loop(0, faces // 8, gather, 0)

    lane = lax.broadcasted_iota(jnp.int32, (LANES, LANES), 1)
    force = []
    warm = []
    for part in range(faces // LANES):
        at = slice(part * LANES, (part + 1) * LANES)
        low = jnp.broadcast_to(low_ref[part : part + 1, :], (LANES, LANES)).T
        index = (low + (lane & (HALF - 1))) & (LANES - 1)
        window = [jnp.take_along_axis(rows[c, at, :], index, axis=1) for c in range(3)]
        force.append(jnp.where(lane < HALF, window[0], window[1]))
        warm.append(window[2])
    force = jnp.concatenate(force, axis=0)
    warm = jnp.concatenate(warm, axis=0)

    def solve(value):
        out = dot(jnp.concatenate(pieces(value, 2), axis=1), table, NT)
        return out[:, 0:LANES] + out[:, LANES : 2 * LANES]

    speed = solve(force)
    for step in range(PICARD):
        square = speed * speed
        damping = DRAG_COEF * lax.rsqrt(1.0 + square + pltpu.roll(square, HALF, 1))
        rest = force - damping * speed
        if step < PICARD - 1:
            speed = solve(rest)
    speed_rows[...] = dot3(top, pieces(rest, 2), NT)
    fluid_top = dot3(top, pieces(warm, 2), NT)[0:1]
    conduct = coef_ref[0:1, :]
    viscosity = coef_ref[1:2, :]

    spread = []
    for value in (conduct * fluid_top, conduct):
        spread += [(choose * part.astype(F32)).astype(BF16) for part in pieces(value, 3)]
    spread.append(choose_b)
    packed = dot(jnp.concatenate(spread, axis=0), place_b, NT)
    packed = [packed[k * devices : (k + 1) * devices] for k in range(7)]
    reply[pl.ds(0, devices, stride=8), :] = packed[0] + (packed[1] + packed[2])
    reply[pl.ds(1, devices, stride=8), :] = packed[3] + (packed[4] + packed[5])
    reply[pl.ds(2, devices, stride=8), :] = packed[6]
    for j in range(3, 8):
        reply[pl.ds(j, devices, stride=8), :] = jnp.zeros((devices, LANES), F32)

    def reply_start(p, s):
        index = p * n_span + s
        pltpu.make_async_remote_copy(
            src_ref=reply.at[pl.ds(pl.multiple_of(index * 8, 8), 8), :],
            dst_ref=reply_got.at[mine, :],
            send_sem=tile_send.at[1], recv_sem=tile_recv.at[1],
            device_id=(p, s), device_id_type=MESH,
        ).start()

    each_peer(reply_start)
    reply_got[mine, :] = reply[mine, :]

    def tiles_wait(k, src, dst):
        many = pl.ds(0, (devices - 1) * 8)
        pltpu.make_async_remote_copy(
            src_ref=src.at[many, :], dst_ref=dst.at[many, :],
            send_sem=tile_send.at[k], recv_sem=tile_recv.at[k],
            device_id=(wrap(pitch + 1, n_pitch), span), device_id_type=MESH,
        ).wait()

    fluid_factor = 1.0 - ALPHA_FLUID * g_smem[0, 0]
    metal_factor = 1.0 - BETA_METAL * metal_smem[0, 0]
    tiles_wait(0, reply, offer_got)
    thrice = jnp.concatenate([choose_b] * 3, axis=0)

    def from_owner(j):
        parts = pieces(offer_got[pl.ds(j, devices, stride=8), :], 3)
        return jnp.sum(
            dot(jnp.concatenate(parts, axis=0), thrice, TN) * place, axis=0, keepdims=True
        )

    metal_top = from_owner(0)
    conduct_metal = from_owner(1)
    wall_temp = (conduct * fluid_top + conduct_metal * metal_top) / (
        conduct * fluid_factor + conduct_metal * metal_factor
    )
    heat = conduct * (fluid_top - fluid_factor * wall_temp)
    cell = cell_ref[...]
    at_pitch = onehot(cell // span_cells, pitch_cells)
    at_span = onehot(lax.rem(cell, span_cells), span_cells).astype(BF16)
    fluxes = (viscosity * speed_rows[0:1, :], viscosity * speed_rows[1:2, :], heat)
    split = [pieces(v, 3) for v in fluxes]
    blank = jnp.zeros(at_pitch.shape, BF16)
    stack = []
    for k in range(3):
        stack += [(at_pitch * s[k].astype(F32)).astype(BF16) for s in split] + [blank]
    total = dot(at_span, jnp.concatenate(stack, axis=0), NT)
    wide = 4 * pitch_cells
    wall_ref[...] = -TIME_STEP * (
        total[:, 0:wide] + (total[:, wide : 2 * wide] + total[:, 2 * wide : 3 * wide])
    )

    tiles_wait(1, reply, reply_got)
    for t in range(slot_dev // LANES):
        tile = reply_got[t * per_tile * 8 : t * per_tile * 8 + 8, :]
        for k in range(t * per_tile + 1, (t + 1) * per_tile):
            tile = tile + reply_got[k * 8 : k * 8 + 8, :]
        slot_rows[:, t * LANES : (t + 1) * LANES] = tile
    metal_k = offer[1:2, :]
    used = slot_rows[2:3, :]
    temp = (slot_rows[0:1, :] + metal_k * offer[0:1, :]) / (
        slot_rows[1:2, :] * fluid_factor + metal_k * metal_factor + (1.0 - used)
    )
    metal_out_ref[...] = jnp.where(
        used > 0.5, free + BETA_METAL * metal_inv_ref[:, 0:1] * temp, old
    )

    up.wait()
    down.wait()

    @pl.when(span < n_span - 1)
    def _():
        right.wait_send()

    @pl.when(span > 0)
    def _():
        left.wait_send()

    @pl.when(span > 0)
    def _():
        right.wait_recv()

    @pl.when(span < n_span - 1)
    def _():
        left.wait_recv()


def advance_kernel(
    x_ref,
    prev_ref,
    next_ref,
    pitch_ref,
    span_ref,
    wall_ref,
    metal_ref,
    out_ref,
    metal_out_ref,
):
    comp = pl.program_id(0)
    part = pl.program_id(1)
    parts = pl.num_programs(1)
    chunk, span_cells, normal = x_ref.shape[1:]
    pitch_cells = wall_ref.shape[1] // 4

    @pl.when((comp == 0) & (part == 0))
    def _():
        metal_out_ref[...] = metal_ref[...]

    weight = TIME_STEP * DIFFUSION
    drift = TIME_STEP * ADVECTION * 0.5
    row = lax.broadcasted_iota(jnp.int32, (span_cells, normal), 0)
    lane = lax.broadcasted_iota(jnp.int32, (span_cells, normal), 1)
    lane_one = lax.broadcasted_iota(jnp.int32, (span_cells, LANES), 1)
    before = jnp.where(part == 0, pitch_ref[0, 0], prev_ref[0, 0])
    after = jnp.where(part == parts - 1, pitch_ref[1, 0], next_ref[0, 0])
    for p in range(chunk):
        here = x_ref[0, p]
        prev = before if p == 0 else x_ref[0, p - 1]
        post = after if p == chunk - 1 else x_ref[0, p + 1]
        span_prev = jnp.where(row == 0, span_ref[0, 0, p : p + 1, :], pltpu.roll(here, 1, 0))
        span_next = jnp.where(
            row == span_cells - 1, span_ref[1, 0, p : p + 1, :], pltpu.roll(here, span_cells - 1, 0)
        )
        down = jnp.where(lane == 0, here, pltpu.roll(here, 1, 1))
        up = jnp.where(lane == normal - 1, here, pltpu.roll(here, normal - 1, 1))
        value = (
            (1.0 - 6.0 * weight) * here
            + (weight - drift) * post
            + (weight + drift) * prev
            + weight * ((span_prev + span_next) + (down + up))
        )
        out_ref[0, p] = value
        column = comp * pitch_cells + part * chunk + p
        source = pltpu.roll(wall_ref[...], lax.rem(LANES - column, LANES), 1)
        out_ref[0, p, :, 0:LANES] += jnp.where(lane_one == 0, source, 0.0)


def vmem():
    return pl.BlockSpec(memory_space=pltpu.VMEM)


def smem():
    return pl.BlockSpec(memory_space=pltpu.SMEM)


def local(
    n_pitch,
    n_span,
    flow_state,
    wall_inverse,
    metal_inverse,
    metal_state,
    metal_conduct,
    face_coef,
    owner_map,
    face_cell,
    sample_col,
    sample_low,
):
    devices = n_pitch * n_span
    comps, pitch_cells, span_cells, normal = flow_state.shape
    slot_dev = metal_state.shape[1]
    per_peer = slot_dev // devices
    faces = owner_map.shape[0]
    any_space = pl.BlockSpec(memory_space=pl.ANY)

    wall, metal_new, pitch_halo, span_halo = pl.pallas_call(
        functools.partial(sample_kernel, n_pitch, n_span, per_peer, span_cells),
        out_shape=(
            jax.ShapeDtypeStruct((span_cells, 4 * pitch_cells), F32),
            jax.ShapeDtypeStruct(metal_state.shape, F32),
            jax.ShapeDtypeStruct((2, comps, span_cells, normal), F32),
            jax.ShapeDtypeStruct((2, comps, pitch_cells, normal), F32),
        ),
        in_specs=[smem()] * 4 + [any_space] + [vmem()] * 8,
        out_specs=[vmem()] * 4,
        scratch_shapes=[
            pltpu.VMEM((comps, 2, pitch_cells * span_cells, LANES), F32),
            pltpu.VMEM((3, faces, LANES), F32),
            pltpu.VMEM((LANES, LANES), F32),
            pltpu.VMEM((8, faces), F32),
            pltpu.VMEM((2, comps, pitch_cells, normal), F32),
            pltpu.VMEM((8, slot_dev), F32),
            pltpu.VMEM((devices * 8, LANES), F32),
            pltpu.VMEM((devices * 8, LANES), F32),
            pltpu.VMEM((devices * 8, LANES), F32),
            pltpu.VMEM((8, slot_dev), F32),
            pltpu.SemaphoreType.DMA((comps, 2)),
            pltpu.SemaphoreType.DMA((2,)),
            pltpu.SemaphoreType.DMA((2,)),
            pltpu.SemaphoreType.DMA((4,)),
            pltpu.SemaphoreType.DMA((4,)),
        ],
        compiler_params=pltpu.CompilerParams(
            collective_id=0, has_side_effects=True, vmem_limit_bytes=VMEM_LIMIT
        ),
        name="sample_faces",
    )(
        sample_col,
        sample_low,
        wall_inverse,
        metal_inverse,
        flow_state.reshape(comps, pitch_cells * span_cells, normal),
        sample_low.reshape(faces // LANES, LANES),
        owner_map.reshape(1, faces),
        face_cell.reshape(1, faces),
        face_coef,
        wall_inverse,
        metal_inverse,
        metal_state,
        metal_conduct.reshape(1, slot_dev),
    )

    chunk = pitch_cells // 2
    new_state, metal_out = pl.pallas_call(
        advance_kernel,
        grid=(comps, 2),
        out_shape=(
            jax.ShapeDtypeStruct(flow_state.shape, F32),
            jax.ShapeDtypeStruct(metal_state.shape, F32),
        ),
        in_specs=[
            pl.BlockSpec((1, chunk, span_cells, normal), lambda c, i: (c, i, 0, 0)),
            pl.BlockSpec(
                (1, 1, span_cells, normal),
                lambda c, i: (c, lax.rem(i * chunk + pitch_cells - 1, pitch_cells), 0, 0),
            ),
            pl.BlockSpec(
                (1, 1, span_cells, normal),
                lambda c, i: (c, lax.rem((i + 1) * chunk, pitch_cells), 0, 0),
            ),
            pl.BlockSpec((2, 1, span_cells, normal), lambda c, i: (0, c, 0, 0)),
            pl.BlockSpec((2, 1, chunk, normal), lambda c, i: (0, c, i, 0)),
            vmem(),
            vmem(),
        ],
        out_specs=[
            pl.BlockSpec((1, chunk, span_cells, normal), lambda c, i: (c, i, 0, 0)),
            pl.BlockSpec(metal_state.shape, lambda c, i: (0, 0)),
        ],
        compiler_params=pltpu.CompilerParams(vmem_limit_bytes=VMEM_LIMIT),
        name="advance",
    )(
        flow_state,
        flow_state,
        flow_state,
        pitch_halo,
        span_halo,
        wall,
        metal_new,
    )
    return (new_state, metal_out)


def solution(mesh):
    return jax.shard_map(
        functools.partial(local, mesh.shape["pitch"], mesh.shape["span"]),
        mesh=mesh,
        in_specs=(
            P(None, "pitch", "span", None),
            P(),
            P(),
            P(None, ("pitch", "span")),
            P(("pitch", "span")),
            P(None, ("pitch", "span")),
            P(("pitch", "span"), None),
            P(("pitch", "span")),
            P(("pitch", "span")),
            P(("pitch", "span")),
        ),
        out_specs=(P(None, "pitch", "span", None), P(None, ("pitch", "span"))),
        check_vma=False,
    )
```

time: 56.5 us -> 35.8 us (0.63)
  Pallas kernels: 50.6 us -> 34.7 us
  local copies, waits for them, and re-layouts: 4.78 us -> 0 us
    pallas_call x3 -> x2, Pallas kernels: 50.6 us -> 34.7 us  [the longest x1 23.2 us: local(): pl.pallas_call(functools.partial(sample_kernel, n_pitch, n_span, per_peer...]
    reshape x3 -> x0, local copies, waits for them, and re-layouts: 4.78 us -> none  [the longest x1 1.72 us: local(): return (new_state, metal_out.reshape(order, slot_dev))]
where the time goes in v1:
time: 35.8 us; the launch traced here: 35.4 us
  Pallas kernels  34.7 us (97%)
  between operations  0.64 us (2%)
    pallas_call x1, Pallas kernels, local(): pl.pallas_call(functools.partial(sample_kernel, n_pitch, n_span, per_peer...  23.2 us
    pallas_call x1, Pallas kernels, local(): pl.pallas_call(advance_kernel, grid=(comps, 2), out_shape=(jax.ShapeDtype...  11.6 us

profile of v1, /device:TPU:0, one launch (start us, length us, event | category | flops | bytes accessed | tf_op | source)
XLA Modules:
  0.0 35.4 jit_solution(3393921846424986093)
XLA Ops:
  0.6 23.2 %sample_faces.1 = (f32[64,128]{1,0:T(8,128)}, f32[16,2048]{1,0:T(8,128)}, f32[2,4,64,256]{3,2,1,0:T(8,128)}, f32[2,4,32,256]{3,2,1,0:T(8,128)}) custom-call(s32[1024]{0:T(1024)} %col_ref.1, s32[1024]{0:T(1024)} %low_smem.1, f32[64,64]{1,0:T(8,128)} %g_ref.1, f32[16,16]{1,0:T(8,128)} %metal_inv_ref.1, f32[4,2048,256]{2,1,0:T(8,128)} %bitcast.5, ...), custom_call_target="tpu_custom_call" | custom-call | tf_op jit(solution)/shard_map/sample_faces/pallas_call | solution.py:457
  23.8 11.6 %advance.1 = (f32[4,32,64,256]{3,2,1,0:T(8,128)}, f32[16,2048]{1,0:T(8,128)}) custom-call(f32[4,32,64,256]{3,2,1,0:T(8,128)} %next_ref.1, f32[4,32,64,256]{3,2,1,0:T(8,128)} %next_ref.1, f32[4,32,64,256]{3,2,1,0:T(8,128)} %next_ref.1, f32[2,4,64,256]{3,2,1,0:T(8,128)} %get-tuple-element.6.pitch_ref, f32[2,4,32,256]{3,2,1,0:T(8,128)} %get-tuple-element.7.span_ref, ...), custom_call_target="tpu_custom_call" | custom-call | tf_op jit(solution)/shard_map/advance/pallas_call | solution.py:505

commit v2 on v1

--- a/solution.py
+++ b/solution.py
@@ -95,7 +95,7 @@
     comps = x_ref.shape[0]
     columns = x_ref.shape[1]
     pitch_cells = columns // span_cells
-    faces = rows.shape[1]
+    faces = rows.shape[0] // 8
     slot_dev = metal_ref.shape[1]
     per_tile = LANES // per_peer
     barrier = pltpu.get_barrier_semaphore()
@@ -120,7 +120,9 @@
     )
     loads = [
         pltpu.make_async_copy(
-            x_ref.at[c, :, pl.ds(t * LANES, LANES)], xv.at[c, t], load_sem.at[c, t]
+            x_ref.at[c, :, pl.ds(t * LANES, LANES)],
+            xv.at[pl.ds((c * 2 + t) * columns, columns), :],
+            load_sem.at[c, t],
         )
         for c in range(comps)
         for t in range(2)
@@ -208,10 +210,11 @@
 
     for side in range(2):
         for c in range(comps):
-            for p in range(pitch_cells):
-                at = p * span_cells + side * (span_cells - 1)
-                for t in range(2):
-                    edges[side, c, p : p + 1, t * LANES : (t + 1) * LANES] = xv[c, t, at : at + 1, :]
+            for t in range(2):
+                at = (c * 2 + t) * columns + side * (span_cells - 1)
+                edges[side, c, :, t * LANES : (t + 1) * LANES] = xv[
+                    pl.ds(at, pitch_cells, stride=span_cells), :
+                ]
 
     @pl.when(span < n_span - 1)
     def _():
@@ -229,20 +232,11 @@
     def _():
         span_ref[1] = jnp.zeros(span_ref.shape[1:], F32)
 
-    lane_row = lax.broadcasted_iota(jnp.int32, (1, LANES), 1)
-
     def gather(group, carry):
-        base = pl.multiple_of(group * 8, 8)
+        base = group * 8
         for k in range(8):
-            col = col_ref[base + k]
-            low = low_smem[base + k]
-            near = low >> 7
-            far = (low + HALF - 1) >> 7
-            keep = lane_row >= (low & (LANES - 1))
-            for c in range(3):
-                rows[c, pl.ds(base + k, 1), :] = jnp.where(
-                    keep, xv[c, near, pl.ds(col, 1), :], xv[c, far, pl.ds(col, 1), :]
-                )
+            at = pl.multiple_of((base + k) * 8, 8)
+            rows[pl.ds(at, 8), :] = xv[pl.ds(col_ref[base + k], 8, stride=columns), :]
         return carry
 
     lax.fori_loop(0, faces // 8, gather, 0)
@@ -251,10 +245,14 @@
     force = []
     warm = []
     for part in range(faces // LANES):
-        at = slice(part * LANES, (part + 1) * LANES)
         low = jnp.broadcast_to(low_ref[part : part + 1, :], (LANES, LANES)).T
         index = (low + (lane & (HALF - 1))) & (LANES - 1)
-        window = [jnp.take_along_axis(rows[c, at, :], index, axis=1) for c in range(3)]
+        near = lane >= low
+        window = []
+        for c in range(3):
+            first = rows[pl.ds(part * LANES * 8 + c * 2, LANES, stride=8), :]
+            second = rows[pl.ds(part * LANES * 8 + c * 2 + 1, LANES, stride=8), :]
+            window.append(jnp.take_along_axis(jnp.where(near, first, second), index, axis=1))
         force.append(jnp.where(lane < HALF, window[0], window[1]))
         warm.append(window[2])
     force = jnp.concatenate(force, axis=0)
@@ -385,6 +383,8 @@
     metal_ref,
     out_ref,
     metal_out_ref,
+    band,
+    mixed,
 ):
     comp = pl.program_id(0)
     part = pl.program_id(1)
@@ -398,8 +398,23 @@
 
     weight = TIME_STEP * DIFFUSION
     drift = TIME_STEP * ADVECTION * 0.5
-    row = lax.broadcasted_iota(jnp.int32, (span_cells, normal), 0)
-    lane = lax.broadcasted_iota(jnp.int32, (span_cells, normal), 1)
+
+    @pl.when((comp == 0) & (part == 0))
+    def _():
+        i = lax.broadcasted_iota(jnp.int32, (normal, normal), 0)
+        j = lax.broadcasted_iota(jnp.int32, (normal, normal), 1)
+        apart = jnp.abs(i - j)
+        end = (i == 0) | (i == normal - 1)
+        centre = (1.0 - 6.0 * weight) / weight
+        diagonal = jnp.where(end, centre + 1.0, centre)
+        one = jnp.where(apart == 1, 1.0, jnp.where(apart == 0, diagonal, 0.0)).astype(BF16)
+        band[0:normal, :] = one
+        band[normal : 2 * normal, :] = one
+
+    split = pieces(x_ref[0].reshape(chunk * span_cells, normal), 2)
+    mixed[...] = dot(jnp.concatenate(split, axis=1), band[...], NN)
+
+    row = lax.broadcasted_iota(jnp.int32, (8, normal), 0)
     lane_one = lax.broadcasted_iota(jnp.int32, (span_cells, LANES), 1)
     before = jnp.where(part == 0, pitch_ref[0, 0], prev_ref[0, 0])
     after = jnp.where(part == parts - 1, pitch_ref[1, 0], next_ref[0, 0])
@@ -407,22 +422,22 @@
         here = x_ref[0, p]
         prev = before if p == 0 else x_ref[0, p - 1]
         post = after if p == chunk - 1 else x_ref[0, p + 1]
-        span_prev = jnp.where(row == 0, span_ref[0, 0, p : p + 1, :], pltpu.roll(here, 1, 0))
-        span_next = jnp.where(
-            row == span_cells - 1, span_ref[1, 0, p : p + 1, :], pltpu.roll(here, span_cells - 1, 0)
+        span_prev = pltpu.roll(here, 1, 0)
+        first = jnp.where(row == 0, span_ref[0, 0, p : p + 1, :], span_prev[0:8])
+        span_prev = jnp.concatenate([first, span_prev[8:]], axis=0)
+        span_next = pltpu.roll(here, span_cells - 1, 0)
+        last = jnp.where(row == 7, span_ref[1, 0, p : p + 1, :], span_next[span_cells - 8 :])
+        span_next = jnp.concatenate([span_next[: span_cells - 8], last], axis=0)
+        near = mixed[p * span_cells : (p + 1) * span_cells, :]
+        value = (
+            (weight - drift) * post
+            + (weight + drift) * prev
+            + weight * ((span_prev + span_next) + near)
         )
-        down = jnp.where(lane == 0, here, pltpu.roll(here, 1, 1))
-        up = jnp.where(lane == normal - 1, here, pltpu.roll(here, normal - 1, 1))
-        value = (
-            (1.0 - 6.0 * weight) * here
-            + (weight - drift) * post
-            + (weight + drift) * prev
-            + weight * ((span_prev + span_next) + (down + up))
-        )
-        out_ref[0, p] = value
         column = comp * pitch_cells + part * chunk + p
         source = pltpu.roll(wall_ref[...], lax.rem(LANES - column, LANES), 1)
-        out_ref[0, p, :, 0:LANES] += jnp.where(lane_one == 0, source, 0.0)
+        out_ref[0, p, :, 0:LANES] = value[:, 0:LANES] + jnp.where(lane_one == 0, source, 0.0)
+        out_ref[0, p, :, LANES:normal] = value[:, LANES:normal]
 
 
 def vmem():
@@ -465,8 +480,8 @@
         in_specs=[smem()] * 4 + [any_space] + [vmem()] * 8,
         out_specs=[vmem()] * 4,
         scratch_shapes=[
-            pltpu.VMEM((comps, 2, pitch_cells * span_cells, LANES), F32),
-            pltpu.VMEM((3, faces, LANES), F32),
+            pltpu.VMEM((comps * 2 * pitch_cells * span_cells, LANES), F32),
+            pltpu.VMEM((faces * 8, LANES), F32),
             pltpu.VMEM((LANES, LANES), F32),
             pltpu.VMEM((8, faces), F32),
             pltpu.VMEM((2, comps, pitch_cells, normal), F32),
@@ -528,6 +543,10 @@
             pl.BlockSpec((1, chunk, span_cells, normal), lambda c, i: (c, i, 0, 0)),
             pl.BlockSpec(metal_state.shape, lambda c, i: (0, 0)),
         ],
+        scratch_shapes=[
+            pltpu.VMEM((2 * normal, normal), BF16),
+            pltpu.VMEM((chunk * span_cells, normal), F32),
+        ],
         compiler_params=pltpu.CompilerParams(vmem_limit_bytes=VMEM_LIMIT),
         name="advance",
     )(

time: 35.8 us -> 36 us (level)
    pallas_call x1, Pallas kernels: 23.2 us -> 24 us  [local(): pl.pallas_call(functools.partial(sample_kernel, n_pitch, n_span, per_peer...]
    pallas_call x1, Pallas kernels: 11.6 us -> 11 us  [local(): pl.pallas_call(advance_kernel, grid=(comps, 2), out_shape=(jax.ShapeDtype...]
where the time goes in v2:
time: 36 us; the launch traced here: 35.6 us
  Pallas kernels  35 us (97%)
  between operations  0.64 us (2%)
    pallas_call x1, Pallas kernels, local(): pl.pallas_call(functools.partial(sample_kernel, n_pitch, n_span, per_peer...  24 us
    pallas_call x1, Pallas kernels, local(): pl.pallas_call(advance_kernel, grid=(comps, 2), out_shape=(jax.ShapeDtype...  11 us

profile of v2, /device:TPU:0, one launch (start us, length us, event | category | flops | bytes accessed | tf_op | source)
XLA Modules:
  0.0 35.6 jit_solution(14650186914803875249)
XLA Ops:
  0.6 24.0 %sample_faces.1 = (f32[64,128]{1,0:T(8,128)}, f32[16,2048]{1,0:T(8,128)}, f32[2,4,64,256]{3,2,1,0:T(8,128)}, f32[2,4,32,256]{3,2,1,0:T(8,128)}) custom-call(s32[1024]{0:T(1024)} %col_ref.1, s32[1024]{0:T(1024)} %low_smem.1, f32[64,64]{1,0:T(8,128)} %g_ref.1, f32[16,16]{1,0:T(8,128)} %metal_inv_ref.1, f32[4,2048,256]{2,1,0:T(8,128)} %bitcast.5, ...), custom_call_target="tpu_custom_call" | custom-call | tf_op jit(solution)/shard_map/sample_faces/pallas_call | solution.py:472
  24.6 11.0 %advance.1 = (f32[4,32,64,256]{3,2,1,0:T(8,128)}, f32[16,2048]{1,0:T(8,128)}) custom-call(f32[4,32,64,256]{3,2,1,0:T(8,128)} %next_ref.1, f32[4,32,64,256]{3,2,1,0:T(8,128)} %next_ref.1, f32[4,32,64,256]{3,2,1,0:T(8,128)} %next_ref.1, f32[2,4,64,256]{3,2,1,0:T(8,128)} %get-tuple-element.6.pitch_ref, f32[2,4,32,256]{3,2,1,0:T(8,128)} %get-tuple-element.7.span_ref, ...), custom_call_target="tpu_custom_call" | custom-call | tf_op jit(solution)/shard_map/advance/pallas_call | solution.py:520
